TPU v7x, 512 devices: a whole 4x4x16 slice. The times are simulated.
512 devices in a mesh: seq: 512 (over y, z, x, core).
Axes of the slice: x: 4, y: 4, z: 16, core: 2. Of those that a mesh axis runs over, the one named last changes fastest.
Arguments:
- inputs: bfloat16 [65536, 768], P('seq'), may hold values from -6 to 6
- first_norm_gain: float32 [768], replicated, may hold values from 0.5 to 2
- first_kernel_weights: bfloat16 [3, 768, 768], replicated, may hold values from -0.125 to 0.125
- first_expand_weight: bfloat16 [768, 768], replicated, may hold values from -0.21875 to 0.21875
- first_project_weight: bfloat16 [768, 768], replicated, may hold values from -0.21875 to 0.21875
- second_norm_gain: float32 [768], replicated, may hold values from 0.5 to 2
- second_kernel_weights: bfloat16 [3, 768, 768], replicated, may hold values from -0.125 to 0.125
- second_expand_weight: bfloat16 [768, 768], replicated, may hold values from -0.21875 to 0.21875
- second_project_weight: bfloat16 [768, 768], replicated, may hold values from -0.21875 to 0.21875
- cotangent: bfloat16 [65536, 768], P('seq'), may hold values from -6 to 6
Outputs:
- outputs: bfloat16 [65536, 768], P('seq')
- input_gradient_rows: bfloat16 [65536, 768], P('seq')
All inputs are finite; a program needn't handle non-finite values.
Results may differ from a plain program's by a relative error of at most 0.02.
Values may be sent and summed in bfloat16 or wider, within the bound.
A program may use at most 64 MiB of HBM per device.

v0:
```python
import jax
import jax.numpy as jnp
from jax import lax
from jax.sharding import PartitionSpec as P


def passed_along(block, axis, distance):
    devices = range(lax.axis_size(axis))
    route = [(i - distance, i) for i in devices if i - distance in devices]
    return lax.ppermute(block, axis, route)


def gelu_back(point, grad):
    return jax.vjp(jax.nn.gelu, point)[1](grad)[0]


def fetch_rows(values, steps):
    return passed_along(values, "seq", steps)


def residual_block_forward(inputs, gain, taps, w_mid, w_out, steps):
    wide = inputs.astype(jnp.float32)
    inv = jax.lax.rsqrt(jnp.mean(wide * wide, axis=-1, keepdims=True) + 1e-06)
    normed = (wide * inv * gain).astype(jnp.bfloat16)
    earlier = fetch_rows(normed, steps)
    later = fetch_rows(normed, -steps)
    pre = jnp.dot(normed, taps[1], preferred_element_type=jnp.float32)
    pre = pre + jnp.dot(earlier, taps[0], preferred_element_type=jnp.float32)
    pre = pre + jnp.dot(later, taps[2], preferred_element_type=jnp.float32)
    act = jax.nn.gelu(pre).astype(jnp.bfloat16)
    mid = jnp.dot(act, w_mid, preferred_element_type=jnp.float32)
    hid = jax.nn.gelu(mid).astype(jnp.bfloat16)
    result = (wide + jnp.dot(hid, w_out, preferred_element_type=jnp.float32)).astype(jnp.bfloat16)
    return (result, (wide, inv, pre, mid))


def residual_block_backward(grad_out, saved, gain, taps, w_mid, w_out, steps):
    wide, inv, pre, mid = saved
    grad_hid = jnp.dot(grad_out, w_out.T, preferred_element_type=jnp.float32)
    grad_mid = gelu_back(mid, grad_hid).astype(jnp.bfloat16)
    grad_act = jnp.dot(grad_mid, w_mid.T, preferred_element_type=jnp.float32)
    grad_pre = gelu_back(pre, grad_act).astype(jnp.bfloat16)
    grad_norm = jnp.dot(grad_pre, taps[1].T, preferred_element_type=jnp.float32)
    for offset, index in ((-steps, 0), (steps, 2)):
        moved = passed_along(grad_pre, "seq", offset)
        grad_norm = grad_norm + jnp.dot(moved, taps[index].T, preferred_element_type=jnp.float32)
    scaled = gain * grad_norm
    back = inv * scaled - wide * inv**3 * jnp.mean(wide * scaled, axis=-1, keepdims=True)
    return (grad_out.astype(jnp.float32) + back).astype(jnp.bfloat16)


def per_device(
    inputs,
    first_norm_gain,
    first_kernel_weights,
    first_expand_weight,
    first_project_weight,
    second_norm_gain,
    second_kernel_weights,
    second_expand_weight,
    second_project_weight,
    cotangent,
):
    near_steps = 2
    far_steps = lax.axis_size("seq") // 16
    leading_block, first_block_residuals = residual_block_forward(
        inputs,
        first_norm_gain,
        first_kernel_weights,
        first_expand_weight,
        first_project_weight,
        near_steps,
    )
    outputs, second_block_residuals = residual_block_forward(
        leading_block,
        second_norm_gain,
        second_kernel_weights,
        second_expand_weight,
        second_project_weight,
        far_steps,
    )
    leading_block_gradient = residual_block_backward(
        cotangent,
        second_block_residuals,
        second_norm_gain,
        second_kernel_weights,
        second_expand_weight,
        second_project_weight,
        far_steps,
    )
    input_gradient_rows = residual_block_backward(
        leading_block_gradient,
        first_block_residuals,
        first_norm_gain,
        first_kernel_weights,
        first_expand_weight,
        first_project_weight,
        near_steps,
    )
    return (outputs, input_gradient_rows)


def solution(mesh):
    return jax.shard_map(
        per_device,
        mesh=mesh,
        in_specs=(P("seq", None), P(), P(), P(), P(), P(), P(), P(), P(), P("seq", None)),
        out_specs=(P("seq", None), P("seq", None)),
        check_vma=False,
    )
```

profile of v0, /device:TPU:24, one launch (start us, length us, event | category | flops | bytes accessed | tf_op | source)
XLA Modules:
  0.0 114.1 jit_solution(13079331185946955774)
XLA Ops:
  0.6 0.0 copy-start
  0.6 1.1 %fusion.61 = f32[128]{0:T(128)S(1)} fusion(bf16[128,768]{1,0:T(8,128)(2,1)} %param.10), kind=kLoop, calls=%fused_computation.83 | loop fusion | flops 294784 | bytes 197120 | tf_op jit(solution)/shard_map/reduce_sum | solution.py:23
  1.8 1.0 fusion.63
  2.9 13.8 %collective-permute-start.1 = (bf16[128,768]{1,0:T(8,128)(2,1)S(1)}, bf16[128,768]{1,0:T(8,128)(2,1)S(1)}, u32[]{:S(2)}, u32[]{:S(2)}) collective-permute-start(bf16[128,768]{1,0:T(8,128)(2,1)S(1)} %fusion.63), channel_id=1, source_target_pairs={{2,0},{3,1},{4,2},{5,3},{6,4},{7,5},{8,6},{9,7},{10,8},{11,9},{12,... | collective-permute-start | bytes 589832 | tf_op jit(solution)/shard_map/ppermute | solution.py:10
  16.6 1.9 %collective-permute-start = (bf16[128,768]{1,0:T(8,128)(2,1)S(1)}, bf16[128,768]{1,0:T(8,128)(2,1)S(1)}, u32[]{:S(2)}, u32[]{:S(2)}) collective-permute-start(bf16[128,768]{1,0:T(8,128)(2,1)S(1)} %fusion.63), channel_id=1, source_target_pairs={{0,2},{1,3},{2,4},{3,5},{4,6},{5,7},{6,8},{7,9},{8,10},{9,11},{10,... | collective-permute-start | bytes 589832 | tf_op jit(solution)/shard_map/ppermute | solution.py:10
  18.6 1.6 %fusion.16 = f32[128,768]{1,0:T(8,128)S(1)} fusion(bf16[128,768]{1,0:T(8,128)(2,1)S(1)} %fusion.63, bf16[3,768,768]{2,1,0:T(8,128)(2,1)} %param.12), kind=kOutput, calls=%fused_computation.26 | convolution fusion | flops 150994944 | bytes 1769472 | tf_op jit(solution)/shard_map/dot_general | solution.py:27
  20.2 8.9 %collective-permute-done = bf16[128,768]{1,0:T(8,128)(2,1)S(1)} collective-permute-done((bf16[128,768]{1,0:T(8,128)(2,1)S(1)}, bf16[128,768]{1,0:T(8,128)(2,1)S(1)}, u32[]{:S(2)}, u32[]{:S(2)}) %collective-permute-start) | collective-permute-done | bytes 196640 | tf_op jit(solution)/shard_map/ppermute | solution.py:10
  29.1 1.6 %convolution_add_fusion.9 = f32[128,768]{1,0:T(8,128)S(1)} fusion(f32[128,768]{1,0:T(8,128)S(1)} %fusion.16, bf16[128,768]{1,0:T(8,128)(2,1)S(1)} %collective-permute-done, bf16[3,768,768]{2,1,0:T(8,128)(2,1)} %param.12), kind=kOutput, calls=%fused_computation.9 | convolution fusion | flops 151093248 | bytes 2162688 | tf_op jit(solution)/shard_map/dot_general | solution.py:28
  30.7 0.0 copy-start.5
  30.7 0.0 collective-permute-done.1
  30.7 0.0 copy-start.2
  30.7 1.7 %convolution_add_fusion.8 = f32[128,768]{1,0:T(8,128)S(1)} fusion(f32[128,768]{1,0:T(8,128)S(1)} %convolution_add_fusion.9, bf16[128,768]{1,0:T(8,128)(2,1)S(1)} %collective-permute-done.1, bf16[3,768,768]{2,1,0:T(8,128)(2,1)} %param.12), kind=kOutput, calls=%fused_computation.8 | convolution fusion | flops 151093248 | bytes 2162688 | tf_op jit(solution)/shard_map/dot_general | solution.py:29
  32.5 0.0 copy-done.5
  32.5 0.0 copy-start.1
  32.5 0.4 fusion.69
  32.8 0.0 copy-done
  32.9 0.0 copy-done.2
  32.9 0.0 copy-start.7
  32.9 0.0 copy-start.10
  32.9 0.5 multiply_reduce_fusion.1
  33.4 0.5 copy-done.10
  33.9 0.1 multiply_convert_fusion.2
  34.0 0.0 copy-done.7
  34.0 4.6 %collective-permute-start.3 = (bf16[128,768]{1,0:T(8,128)(2,1)S(1)}, bf16[128,768]{1,0:T(8,128)(2,1)S(1)}, u32[]{:S(2)}, u32[]{:S(2)}) collective-permute-start(bf16[128,768]{1,0:T(8,128)(2,1)S(1)} %multiply_convert_fusion.2), channel_id=1, source_target_pairs={{32,0},{33,1},{34,2},{35,3},{36,4},{37,5},{38,6},{39,7},{40,8},{41... | collective-permute-start | bytes 589832 | tf_op jit(solution)/shard_map/ppermute | solution.py:10
  38.6 5.2 %collective-permute-start.2 = (bf16[128,768]{1,0:T(8,128)(2,1)S(1)}, bf16[128,768]{1,0:T(8,128)(2,1)S(1)}, u32[]{:S(2)}, u32[]{:S(2)}) collective-permute-start(bf16[128,768]{1,0:T(8,128)(2,1)S(1)} %multiply_convert_fusion.2), channel_id=1, source_target_pairs={{0,32},{1,33},{2,34},{3,35},{4,36},{5,37},{6,38},{7,39},{8,40},{9,... | collective-permute-start | bytes 589832 | tf_op jit(solution)/shard_map/ppermute | solution.py:10
  43.8 0.0 copy-done.1
  43.8 0.3 fusion.8
  44.1 17.3 %collective-permute-done.2 = bf16[128,768]{1,0:T(8,128)(2,1)S(1)} collective-permute-done((bf16[128,768]{1,0:T(8,128)(2,1)S(1)}, bf16[128,768]{1,0:T(8,128)(2,1)S(1)}, u32[]{:S(2)}, u32[]{:S(2)}) %collective-permute-start.2) | collective-permute-done | bytes 196640 | tf_op jit(solution)/shard_map/ppermute | solution.py:10
  61.5 0.3 convolution_add_fusion.6
  61.8 0.0 copy-start.4
  61.8 0.0 collective-permute-done.3
  61.8 0.3 convolution_add_fusion.5
  62.2 0.9 copy-done.4
  63.1 0.0 copy-start.3
  63.1 0.4 fusion.70
  63.4 0.9 copy-done.3
  64.3 0.0 copy-start.8
  64.3 1.0 fusion.20
  65.4 0.0 copy-done.8
  65.4 2.6 %fusion.53 = bf16[128,768]{1,0:T(8,128)(2,1)S(1)} fusion(f32[128,768]{1,0:T(8,128)S(1)} %convolution_add_fusion.5, bf16[768,768]{1,0:T(8,128)(2,1)} %param.17, f32[128,768]{1,0:T(8,128)S(1)} %fusion.70, bf16[128,768]{1,0:T(8,128)(2,1)S(1)} %copy-done.8, bf16[768,768]{1,0:T(8,128)(2,1)} %param.18), kind=kOutput, calls=%fused_computation.75 | convolution fusion | flops 305922048 | bytes 3538944 | tf_op jit(solution)/shard_map/dot_general | solution.py:41
  68.0 1.9 %collective-permute-start.5 = (bf16[128,768]{1,0:T(8,128)(2,1)S(1)}, bf16[128,768]{1,0:T(8,128)(2,1)S(1)}, u32[]{:S(2)}, u32[]{:S(2)}) collective-permute-start(bf16[128,768]{1,0:T(8,128)(2,1)S(1)} %fusion.53), channel_id=1, source_target_pairs={{0,32},{1,33},{2,34},{3,35},{4,36},{5,37},{6,38},{7,39},{8,40},{9,... | collective-permute-start | bytes 589832 | tf_op jit(solution)/shard_map/ppermute | solution.py:10
  70.0 8.7 %collective-permute-start.4 = (bf16[128,768]{1,0:T(8,128)(2,1)S(1)}, bf16[128,768]{1,0:T(8,128)(2,1)S(1)}, u32[]{:S(2)}, u32[]{:S(2)}) collective-permute-start(bf16[128,768]{1,0:T(8,128)(2,1)S(1)} %fusion.53), channel_id=1, source_target_pairs={{32,0},{33,1},{34,2},{35,3},{36,4},{37,5},{38,6},{39,7},{40,8},{41... | collective-permute-start | bytes 589832 | tf_op jit(solution)/shard_map/ppermute | solution.py:10
  78.7 1.8 %fusion.6 = f32[128,768]{1,0:T(8,128)S(1)} fusion(bf16[128,768]{1,0:T(8,128)(2,1)S(1)} %fusion.53, bf16[3,768,768]{2,1,0:T(8,128)(2,1)} %param.16), kind=kOutput, calls=%fused_computation.16 | convolution fusion | flops 150994944 | bytes 1769472 | tf_op jit(solution)/shard_map/dot_general | solution.py:43
  80.5 8.7 %collective-permute-done.4 = bf16[128,768]{1,0:T(8,128)(2,1)S(1)} collective-permute-done((bf16[128,768]{1,0:T(8,128)(2,1)S(1)}, bf16[128,768]{1,0:T(8,128)(2,1)S(1)}, u32[]{:S(2)}, u32[]{:S(2)}) %collective-permute-start.4) | collective-permute-done | bytes 196640 | tf_op jit(solution)/shard_map/ppermute | solution.py:10
  89.2 1.8 %convolution_add_fusion.3 = f32[128,768]{1,0:T(8,128)S(1)} fusion(f32[128,768]{1,0:T(8,128)S(1)} %fusion.6, bf16[128,768]{1,0:T(8,128)(2,1)S(1)} %collective-permute-done.4, bf16[3,768,768]{2,1,0:T(8,128)(2,1)} %param.16), kind=kOutput, calls=%fused_computation.3 | convolution fusion | flops 151093248 | bytes 2162688 | tf_op jit(solution)/shard_map/dot_general | solution.py:46
  91.0 0.0 copy-start.9
  91.0 0.0 collective-permute-done.5
  91.0 1.9 %multiply_reduce_fusion = (f32[128]{0:T(128)S(1)}, f32[128,768]{1,0:T(8,128)S(1)}) fusion(f32[128,768]{1,0:T(8,128)S(1)} %get-tuple-element.7, f32[128,768]{1,0:T(8,128)S(1)} %convolution_add_fusion.3, bf16[128,768]{1,0:T(8,128)(2,1)S(1)} %collective-permute-done.5, bf16[3,768,768]{2,1,0:T(8,128)(2,1)} %param.16, f32[768]{0:T(1024)S(1)} %copy-done.10), kind=kOutput, calls=%fused_computation.92 | convolution fusion | flops 151388032 | bytes 2559488 | tf_op jit(solution)/shard_map/dot_general | solution.py:46
  93.0 0.0 copy-start.6
  93.0 0.0 copy-done.9
  93.0 0.2 add_convert_fusion
  93.2 1.1 copy-done.6
  94.3 2.0 %fusion.39 = bf16[128,768]{1,0:T(8,128)(2,1)S(1)} fusion(f32[128,768]{1,0:T(8,128)S(1)} %convolution_add_fusion.8, bf16[768,768]{1,0:T(8,128)(2,1)S(1)} %copy-done.6, f32[128,768]{1,0:T(8,128)} %copy-done.7, bf16[128,768]{1,0:T(8,128)(2,1)S(1)} %add_convert_fusion, bf16[768,768]{1,0:T(8,128)(2,1)S(1)} %copy-done), kind=kOutput, calls=%fused_computation.61 | convolution fusion | flops 305922048 | bytes 3538944 | tf_op jit(solution)/shard_map/dot_general | solution.py:41
  96.3 1.9 %collective-permute-start.7 = (bf16[128,768]{1,0:T(8,128)(2,1)S(1)}, bf16[128,768]{1,0:T(8,128)(2,1)S(1)}, u32[]{:S(2)}, u32[]{:S(2)}) collective-permute-start(bf16[128,768]{1,0:T(8,128)(2,1)S(1)} %fusion.39), channel_id=1, source_target_pairs={{0,2},{1,3},{2,4},{3,5},{4,6},{5,7},{6,8},{7,9},{8,10},{9,11},{10,... | collective-permute-start | bytes 589832 | tf_op jit(solution)/shard_map/ppermute | solution.py:10
  98.2 8.1 %collective-permute-start.6 = (bf16[128,768]{1,0:T(8,128)(2,1)S(1)}, bf16[128,768]{1,0:T(8,128)(2,1)S(1)}, u32[]{:S(2)}, u32[]{:S(2)}) collective-permute-start(bf16[128,768]{1,0:T(8,128)(2,1)S(1)} %fusion.39), channel_id=1, source_target_pairs={{2,0},{3,1},{4,2},{5,3},{6,4},{7,5},{8,6},{9,7},{10,8},{11,9},{12,... | collective-permute-start | bytes 589832 | tf_op jit(solution)/shard_map/ppermute | solution.py:10
  106.3 1.8 %fusion.14 = f32[128,768]{1,0:T(8,128)S(1)} fusion(bf16[128,768]{1,0:T(8,128)(2,1)S(1)} %fusion.39, bf16[3,768,768]{2,1,0:T(8,128)(2,1)} %param.12), kind=kOutput, calls=%fused_computation.24 | convolution fusion | flops 150994944 | bytes 1769472 | tf_op jit(solution)/shard_map/dot_general | solution.py:43
  108.1 0.0 copy-start.11
  108.1 1.3 %collective-permute-done.6 = bf16[128,768]{1,0:T(8,128)(2,1)S(1)} collective-permute-done((bf16[128,768]{1,0:T(8,128)(2,1)S(1)}, bf16[128,768]{1,0:T(8,128)(2,1)S(1)}, u32[]{:S(2)}, u32[]{:S(2)}) %collective-permute-start.6) | collective-permute-done | bytes 196640 | tf_op jit(solution)/shard_map/ppermute | solution.py:10
  109.5 1.8 %convolution_add_fusion.1 = f32[128,768]{1,0:T(8,128)S(1)} fusion(f32[128,768]{1,0:T(8,128)S(1)} %fusion.14, bf16[128,768]{1,0:T(8,128)(2,1)S(1)} %collective-permute-done.6, bf16[3,768,768]{2,1,0:T(8,128)(2,1)} %param.12), kind=kOutput, calls=%fused_computation.1 | convolution fusion | flops 151093248 | bytes 2162688 | tf_op jit(solution)/shard_map/dot_general | solution.py:46
  111.3 0.0 collective-permute-done.7
  111.3 0.0 copy-done.11
  111.3 1.9 %fusion.68 = (f32[128]{0:T(128)S(1)}, f32[128,768]{1,0:T(8,128)S(1)}) fusion(bf16[128,768]{1,0:T(8,128)(2,1)S(1)} %copy-done.2, f32[128,768]{1,0:T(8,128)S(1)} %convolution_add_fusion.1, bf16[128,768]{1,0:T(8,128)(2,1)S(1)} %collective-permute-done.7, bf16[3,768,768]{2,1,0:T(8,128)(2,1)} %param.12, f32[768]{0:T(1024)S(1)} %copy-done.11), kind=kOutput, calls=%fused_computation.90 | convolution fusion | flops 151486336 | bytes 2362880 | tf_op jit(solution)/shard_map/dot_general | solution.py:46
  113.2 0.9 fusion.67
  (4 shorter events, 0.0 us)
Async XLA Ops:
  0.6 32.2 %copy-start = (bf16[768,768]{1,0:T(8,128)(2,1)S(1)}, bf16[768,768]{1,0:T(8,128)(2,1)}, u32[]{:S(2)}) copy-start(bf16[768,768]{1,0:T(8,128)(2,1)} %param.14) | copy-start | bytes 3538948
  2.9 27.9 %collective-permute-start.1 = (bf16[128,768]{1,0:T(8,128)(2,1)S(1)}, bf16[128,768]{1,0:T(8,128)(2,1)S(1)}, u32[]{:S(2)}, u32[]{:S(2)}) collective-permute-start(bf16[128,768]{1,0:T(8,128)(2,1)S(1)} %fusion.63), channel_id=1, source_target_pairs={{2,0},{3,1},{4,2},{5,3},{6,4},{7,5},{8,6},{9,7},{10,8},{11,9},{12,... | collective-permute-start | bytes 589832 | tf_op jit(solution)/shard_map/ppermute | solution.py:10
  16.6 12.5 %collective-permute-start = (bf16[128,768]{1,0:T(8,128)(2,1)S(1)}, bf16[128,768]{1,0:T(8,128)(2,1)S(1)}, u32[]{:S(2)}, u32[]{:S(2)}) collective-permute-start(bf16[128,768]{1,0:T(8,128)(2,1)S(1)} %fusion.63), channel_id=1, source_target_pairs={{0,2},{1,3},{2,4},{3,5},{4,6},{5,7},{6,8},{7,9},{8,10},{9,11},{10,... | collective-permute-start | bytes 589832 | tf_op jit(solution)/shard_map/ppermute | solution.py:10
  30.7 1.7 %copy-start.5 = (bf16[768,768]{1,0:T(8,128)(2,1)S(1)}, bf16[768,768]{1,0:T(8,128)(2,1)}, u32[]{:S(2)}) copy-start(bf16[768,768]{1,0:T(8,128)(2,1)} %param.13) | copy-start | bytes 3538948
  30.7 2.1 %copy-start.2 = (bf16[128,768]{1,0:T(8,128)(2,1)S(1)}, bf16[128,768]{1,0:T(8,128)(2,1)}, u32[]{:S(2)}) copy-start(bf16[128,768]{1,0:T(8,128)(2,1)} %param.10) | copy-start | bytes 589828
  32.5 11.3 %copy-start.1 = (bf16[3,768,768]{2,1,0:T(8,128)(2,1)S(1)}, bf16[3,768,768]{2,1,0:T(8,128)(2,1)}, u32[]{:S(2)}) copy-start(bf16[3,768,768]{2,1,0:T(8,128)(2,1)} %param.16) | copy-start | bytes 10616836
  32.9 1.1 %copy-start.7 = (f32[128,768]{1,0:T(8,128)}, f32[128,768]{1,0:T(8,128)S(1)}, u32[]{:S(2)}) copy-start(f32[128,768]{1,0:T(8,128)S(1)} %fusion.69) | copy-start | bytes 1179652
  32.9 1.0 copy-start.10
  34.0 27.8 %collective-permute-start.3 = (bf16[128,768]{1,0:T(8,128)(2,1)S(1)}, bf16[128,768]{1,0:T(8,128)(2,1)S(1)}, u32[]{:S(2)}, u32[]{:S(2)}) collective-permute-start(bf16[128,768]{1,0:T(8,128)(2,1)S(1)} %multiply_convert_fusion.2), channel_id=1, source_target_pairs={{32,0},{33,1},{34,2},{35,3},{36,4},{37,5},{38,6},{39,7},{40,8},{41... | collective-permute-start | bytes 589832 | tf_op jit(solution)/shard_map/ppermute | solution.py:10
  38.6 22.9 %collective-permute-start.2 = (bf16[128,768]{1,0:T(8,128)(2,1)S(1)}, bf16[128,768]{1,0:T(8,128)(2,1)S(1)}, u32[]{:S(2)}, u32[]{:S(2)}) collective-permute-start(bf16[128,768]{1,0:T(8,128)(2,1)S(1)} %multiply_convert_fusion.2), channel_id=1, source_target_pairs={{0,32},{1,33},{2,34},{3,35},{4,36},{5,37},{6,38},{7,39},{8,40},{9,... | collective-permute-start | bytes 589832 | tf_op jit(solution)/shard_map/ppermute | solution.py:10
  61.8 1.3 %copy-start.4 = (bf16[768,768]{1,0:T(8,128)(2,1)S(1)}, bf16[768,768]{1,0:T(8,128)(2,1)}, u32[]{:S(2)}) copy-start(bf16[768,768]{1,0:T(8,128)(2,1)} %param.17) | copy-start | bytes 3538948
  63.1 1.3 %copy-start.3 = (bf16[768,768]{1,0:T(8,128)(2,1)S(1)}, bf16[768,768]{1,0:T(8,128)(2,1)}, u32[]{:S(2)}) copy-start(bf16[768,768]{1,0:T(8,128)(2,1)} %param.18) | copy-start | bytes 3538948
  64.3 1.1 copy-start.8
  68.0 23.0 %collective-permute-start.5 = (bf16[128,768]{1,0:T(8,128)(2,1)S(1)}, bf16[128,768]{1,0:T(8,128)(2,1)S(1)}, u32[]{:S(2)}, u32[]{:S(2)}) collective-permute-start(bf16[128,768]{1,0:T(8,128)(2,1)S(1)} %fusion.53), channel_id=1, source_target_pairs={{0,32},{1,33},{2,34},{3,35},{4,36},{5,37},{6,38},{7,39},{8,40},{9,... | collective-permute-start | bytes 589832 | tf_op jit(solution)/shard_map/ppermute | solution.py:10
  70.0 19.2 %collective-permute-start.4 = (bf16[128,768]{1,0:T(8,128)(2,1)S(1)}, bf16[128,768]{1,0:T(8,128)(2,1)S(1)}, u32[]{:S(2)}, u32[]{:S(2)}) collective-permute-start(bf16[128,768]{1,0:T(8,128)(2,1)S(1)} %fusion.53), channel_id=1, source_target_pairs={{32,0},{33,1},{34,2},{35,3},{36,4},{37,5},{38,6},{39,7},{40,8},{41... | collective-permute-start | bytes 589832 | tf_op jit(solution)/shard_map/ppermute | solution.py:10
  91.0 2.0 %copy-start.9 = (bf16[128,768]{1,0:T(8,128)(2,1)S(1)}, bf16[128,768]{1,0:T(8,128)(2,1)}, u32[]{:S(2)}) copy-start(bf16[128,768]{1,0:T(8,128)(2,1)} %param.19) | copy-start | bytes 589828
  93.0 1.3 %copy-start.6 = (bf16[768,768]{1,0:T(8,128)(2,1)S(1)}, bf16[768,768]{1,0:T(8,128)(2,1)}, u32[]{:S(2)}) copy-start(bf16[768,768]{1,0:T(8,128)(2,1)} %param.13) | copy-start | bytes 3538948
  96.3 15.1 %collective-permute-start.7 = (bf16[128,768]{1,0:T(8,128)(2,1)S(1)}, bf16[128,768]{1,0:T(8,128)(2,1)S(1)}, u32[]{:S(2)}, u32[]{:S(2)}) collective-permute-start(bf16[128,768]{1,0:T(8,128)(2,1)S(1)} %fusion.39), channel_id=1, source_target_pairs={{0,2},{1,3},{2,4},{3,5},{4,6},{5,7},{6,8},{7,9},{8,10},{9,11},{10,... | collective-permute-start | bytes 589832 | tf_op jit(solution)/shard_map/ppermute | solution.py:10
  98.2 11.3 %collective-permute-start.6 = (bf16[128,768]{1,0:T(8,128)(2,1)S(1)}, bf16[128,768]{1,0:T(8,128)(2,1)S(1)}, u32[]{:S(2)}, u32[]{:S(2)}) collective-permute-start(bf16[128,768]{1,0:T(8,128)(2,1)S(1)} %fusion.39), channel_id=1, source_target_pairs={{2,0},{3,1},{4,2},{5,3},{6,4},{7,5},{8,6},{9,7},{10,8},{11,9},{12,... | collective-permute-start | bytes 589832 | tf_op jit(solution)/shard_map/ppermute | solution.py:10
  108.1 3.2 %copy-start.11 = (f32[768]{0:T(1024)S(1)}, f32[768]{0:T(1024)}, u32[]{:S(2)}) copy-start(f32[768]{0:T(1024)} %param.11) | copy-start | bytes 9220
where the time goes:
time: 115 us; the launch traced here: 114 us
  starting transfers between devices  46.2 us (40%)
  waiting for transfers between devices  36.3 us (32%)
  matrix products  23.8 us (21%)
  local copies, waits for them, and re-layouts  3.5 us (3%)
  other arithmetic  3.33 us (3%)
    ppermute x8, starting transfers between devices, passed_along(): return lax.ppermute(block, axis, route)  46.2 us
    ppermute x8, waiting for transfers between devices, passed_along(): return lax.ppermute(block, axis, route)  36.3 us
    dot_general x4, matrix products, residual_block_backward(): jnp.dot(moved, taps[index].T, preferred_element_type=jnp.float32)  7.46 us
    dot_general x2, matrix products, residual_block_backward(): grad_act = jnp.dot(grad_mid, w_mid.T, preferred_element_type=jnp.float32)  4.62 us
    dot_general x2, matrix products, residual_block_backward(): grad_norm = jnp.dot(grad_pre, taps[1].T, preferred_element_type=jnp.float32)  3.62 us
    unnamed x24, local copies, waits for them, and re-layouts  3.5 us
  transfers between devices with their start and end apart: 8, of which 4 were waited for; matrix products, arithmetic and copies ran while one was open for 10% of the time, Pallas kernels for 0%

commit v1 on v0

v1 whole, which is shorter than its diff:
```python
import math

import jax
import jax.numpy as jnp
from jax import lax
from jax.experimental import pallas as pl
from jax.experimental.pallas import tpu as pltpu
from jax.sharding import PartitionSpec as P

MESH = pl.DeviceIdType.MESH
C = 768
EPS = 1e-6
CURVE = math.sqrt(2.0 / math.pi)
CUBIC = 0.044715

TAPS = (0, 5)
EXPAND = (3, 8)
PROJECT = (4, 9)

NEAR_FWD, FAR_FWD, FAR_BWD, NEAR_BWD = range(4)


def dot(a, b):
    return jnp.dot(a, b, preferred_element_type=jnp.float32)


def gelu_and_slope(v):
    square = v * v
    t = jnp.tanh(v * (CURVE + (CURVE * CUBIC) * square))
    half = 0.5 + 0.5 * t
    slope = half + (0.5 * v) * (1.0 - t * t) * (CURVE + (3.0 * CURVE * CUBIC) * square)
    return v * half, slope


def make_kernel(devices, near, far, rows, chunks):
    part = rows // chunks
    strides = (near, far, far, near)

    def kernel(
        x_hbm, g1_ref, w1_hbm, m1_hbm, p1_hbm, g2_ref, w2_hbm, m2_hbm, p2_hbm, cot_hbm,
        out_hbm, gin_hbm,
        wts, wts_t, x_v, cot_v, nrm1, nrm2, gp2, gp1, x2, hid2, dy1, out_v, gin_v,
        slope_pre1, slope_mid1, slope_pre2, slope_mid2, own, ghid2, inv1, inv2,
        load_sem, store_sem, send_sem, recv_sem,
    ):
        me = lax.axis_index("seq")
        bufs = (nrm1, nrm2, gp2, gp1)

        def exists(distance):
            return (me + distance >= 0) & (me + distance < devices)

        barrier = pltpu.get_barrier_semaphore()
        partners = (-near, near, -far, far)
        for distance in partners:

            @pl.when(exists(distance))
            def _():
                pl.semaphore_signal(barrier, inc=1, device_id=(me + distance,), device_id_type=MESH)

        def load(i, src, dst):
            return pltpu.make_async_copy(src, dst, load_sem.at[i])

        loads = [load(0, x_hbm, x_v)]
        loads.append(load(1, w1_hbm, wts.at[pl.ds(0, 3)]))
        loads.append(load(2, m1_hbm, wts.at[3]))
        loads.append(load(3, p1_hbm, wts.at[4]))
        loads.append(load(4, cot_hbm, cot_v))
        loads.append(load(5, p2_hbm, wts.at[9]))
        loads.append(load(6, m2_hbm, wts.at[8]))
        loads.append(load(7, w2_hbm, wts.at[pl.ds(5, 3)]))
        for one in loads:
            one.start()

        for stage in range(4):
            for slot, distance in ((0, -strides[stage]), (2, strides[stage])):

                @pl.when(jnp.logical_not(exists(distance)))
                def _():
                    bufs[stage][slot] = jnp.zeros((rows, C), jnp.bfloat16)

        def copies(stage, c):
            stride, buf, at = strides[stage], bufs[stage], span(c)
            for side, (slot, distance) in enumerate(((0, stride), (2, -stride))):
                yield (
                    exists(distance),
                    exists(-distance),
                    pltpu.make_async_remote_copy(
                        src_ref=buf.at[1, at],
                        dst_ref=buf.at[slot, at],
                        send_sem=send_sem.at[stage, side, c],
                        recv_sem=recv_sem.at[stage, side, c],
                        device_id=(me + distance,),
                        device_id_type=MESH,
                    ),
                )

        def span(c):
            return pl.ds(pl.multiple_of(c * part, part), part)

        def send(stage, c):
            for sends, _, copy in copies(stage, c):
                pl.when(sends)(copy.start)

        def receive(stage, c):
            for _, receives, copy in copies(stage, c):
                pl.when(receives)(copy.wait_recv)

        def all_sent(stage):
            def body(c, carry):
                for sends, _, copy in copies(stage, c):
                    pl.when(sends)(copy.wait_send)
                return carry

            lax.fori_loop(0, chunks, body, 0)

        def per_chunk(body):
            def step(c, carry):
                body(c, span(c))
                return carry

            lax.fori_loop(0, chunks, step, 0)

        def transpose(*which):
            for i in which:
                wts_t[i] = wts[i].T

        gain1 = g1_ref[...].reshape(1, C)
        gain2 = g2_ref[...].reshape(1, C)

        def normalize(wide, gain):
            inv = lax.rsqrt(jnp.mean(wide * wide, axis=-1, keepdims=True) + EPS)
            return inv, (wide * inv * gain).astype(jnp.bfloat16)

        loads[0].wait()
        inv, normed = normalize(x_v[...].astype(jnp.float32), gain1)
        inv1[...] = inv
        nrm1[1] = normed
        pl.semaphore_wait(barrier, sum(exists(distance).astype(jnp.int32) for distance in partners))

        def first_send(c, at):
            send(NEAR_FWD, c)

        per_chunk(first_send)
        loads[1].wait()
        own[...] = dot(nrm1[1], wts[1])
        loads[2].wait()
        loads[3].wait()

        def first_forward(c, at):
            receive(NEAR_FWD, c)
            pre = own[at, :] + dot(nrm1[0, at], wts[0]) + dot(nrm1[2, at], wts[2])
            act, slope_pre1[at, :] = gelu_and_slope(pre)
            mid = dot(act.astype(jnp.bfloat16), wts[3])
            hid, slope_mid1[at, :] = gelu_and_slope(mid)
            result = x_v[at, :].astype(jnp.float32) + dot(hid.astype(jnp.bfloat16), wts[4])
            result = result.astype(jnp.bfloat16)
            x2[at, :] = result
            inv, normed = normalize(result.astype(jnp.float32), gain2)
            inv2[at, :] = inv
            nrm2[1, at] = normed
            send(FAR_FWD, c)

        per_chunk(first_forward)

        for i in (4, 5, 6, 7):
            loads[i].wait()
        transpose(9)
        ghid2[...] = dot(cot_v[...], wts_t[9])
        own[...] = dot(nrm2[1], wts[6])
        transpose(8)

        def second_block(c, at):
            receive(FAR_FWD, c)
            pre = own[at, :] + dot(nrm2[0, at], wts[5]) + dot(nrm2[2, at], wts[7])
            act, slope_pre = gelu_and_slope(pre)
            mid = dot(act.astype(jnp.bfloat16), wts[8])
            hid, slope_mid = gelu_and_slope(mid)
            hid2[at, :] = hid.astype(jnp.bfloat16)
            grad_mid = (ghid2[at, :] * slope_mid).astype(jnp.bfloat16)
            grad_act = dot(grad_mid, wts_t[8])
            gp2[1, at] = (grad_act * slope_pre).astype(jnp.bfloat16)
            send(FAR_BWD, c)

            @pl.when(c == 0)
            def _():
                transpose(5, 6, 7)

            @pl.when(c == 1)
            def _():
                transpose(4, 3)

            @pl.when(c == 2)
            def _():
                transpose(0, 1, 2)

        per_chunk(second_block)
        out_v[...] = (x2[...].astype(jnp.float32) + dot(hid2[...], wts[9])).astype(jnp.bfloat16)
        store_out = pltpu.make_async_copy(out_v, out_hbm, store_sem.at[0])
        store_out.start()
        own[...] = dot(gp2[1], wts_t[6])

        def norm_backward(dy, wide, inv, gain, grad_norm):
            scaled = gain * grad_norm
            inner = jnp.mean(wide * scaled, axis=-1, keepdims=True)
            return (dy + (inv * scaled - wide * (inv * inv * inv * inner))).astype(jnp.bfloat16)

        def second_to_first(c, at):
            receive(FAR_BWD, c)
            grad_norm = own[at, :] + dot(gp2[2, at], wts_t[5]) + dot(gp2[0, at], wts_t[7])
            dy = norm_backward(
                cot_v[at, :].astype(jnp.float32), x2[at, :].astype(jnp.float32), inv2[at, :], gain2, grad_norm
            )
            dy1[at, :] = dy
            grad_mid = (dot(dy, wts_t[4]) * slope_mid1[at, :]).astype(jnp.bfloat16)
            gp1[1, at] = (dot(grad_mid, wts_t[3]) * slope_pre1[at, :]).astype(jnp.bfloat16)
            send(NEAR_BWD, c)

        per_chunk(second_to_first)
        own[...] = dot(gp1[1], wts_t[1])

        def first_backward(c, at):
            receive(NEAR_BWD, c)
            grad_norm = own[at, :] + dot(gp1[2, at], wts_t[0]) + dot(gp1[0, at], wts_t[2])
            gin_v[at, :] = norm_backward(
                dy1[at, :].astype(jnp.float32), x_v[at, :].astype(jnp.float32), inv1[at, :], gain1, grad_norm
            )

        per_chunk(first_backward)
        store_gin = pltpu.make_async_copy(gin_v, gin_hbm, store_sem.at[1])
        store_gin.start()
        for stage in range(4):
            all_sent(stage)
        store_out.wait()
        store_gin.wait()

    return kernel


def solution(mesh):
    devices = mesh.shape["seq"]
    chunks = 4

    def per_device(x, g1, w1, m1, p1, g2, w2, m2, p2, cot):
        rows = x.shape[0]
        span = devices * rows
        near, far = 256 // rows, 4096 // rows
        assert span == 65536
        bf16 = lambda *lead: pltpu.VMEM((*lead, rows, C), jnp.bfloat16)
        f32 = lambda: pltpu.VMEM((rows, C), jnp.float32)
        whole = pl.BlockSpec(memory_space=pl.ANY)
        vmem = pl.BlockSpec(memory_space=pltpu.VMEM)
        block = jax.ShapeDtypeStruct((rows, C), jnp.bfloat16)
        results = pl.pallas_call(
            make_kernel(devices, near, far, rows, chunks),
            out_shape=(block, block),
            in_specs=[whole, vmem, whole, whole, whole, vmem, whole, whole, whole, whole],
            out_specs=(whole, whole),
            scratch_shapes=[
                pltpu.VMEM((10, C, C), jnp.bfloat16),
                pltpu.VMEM((10, C, C), jnp.bfloat16),
                bf16(), bf16(), bf16(3), bf16(3), bf16(3), bf16(3), bf16(), bf16(), bf16(), bf16(), bf16(),
                f32(), f32(), f32(), f32(), f32(), f32(),
                pltpu.VMEM((rows, 1), jnp.float32),
                pltpu.VMEM((rows, 1), jnp.float32),
                pltpu.SemaphoreType.DMA((8,)),
                pltpu.SemaphoreType.DMA((2,)),
                pltpu.SemaphoreType.DMA((4, 2, chunks)),
                pltpu.SemaphoreType.DMA((4, 2, chunks)),
            ],
            compiler_params=pltpu.CompilerParams(
                collective_id=0, has_side_effects=True, vmem_limit_bytes=62 << 20
            ),
        )(x, g1, w1, m1, p1, g2, w2, m2, p2, cot)

        def hand_over(a, b, a_out, b_out):
            a_out[...] = a[...]
            b_out[...] = b[...]

        return pl.pallas_call(
            hand_over,
            out_shape=(block, block),
            in_specs=[vmem, vmem],
            out_specs=(vmem, vmem),
            compiler_params=pltpu.CompilerParams(vmem_limit_bytes=62 << 20),
        )(*results)

    return jax.shard_map(
        per_device,
        mesh=mesh,
        in_specs=(P("seq", None), P(), P(), P(), P(), P(), P(), P(), P(), P("seq", None)),
        out_specs=(P("seq", None), P("seq", None)),
        check_vma=False,
    )
```

time: 115 us -> 69.6 us (0.61)
  Pallas kernels: 0 us -> 67.8 us
  starting transfers between devices: 46.2 us -> 0 us
  waiting for transfers between devices: 36.3 us -> 0 us
  matrix products: 23.8 us -> 0 us
  local copies, waits for them, and re-layouts: 3.5 us -> 0 us
  other arithmetic: 3.33 us -> 0 us
    pallas_call x0 -> x2, Pallas kernels: none -> 67.8 us  [the longest x1 66.1 us: per_device(): pl.pallas_call(make_kernel(devices, near, far, rows, chunks), out_shape=(...]
    ppermute x8 -> x0, starting transfers between devices: 46.2 us -> none  [passed_along(): return lax.ppermute(block, axis, route)]
    ppermute x8 -> x0, waiting for transfers between devices: 36.3 us -> none  [passed_along(): return lax.ppermute(block, axis, route)]
    dot_general x18 -> x0, matrix products: 23.8 us -> none  [the longest x4 7.46 us: residual_block_backward(): jnp.dot(moved, taps[index].T, preferred_element_type=jnp.float32)]
    unnamed x24 -> x0, local copies, waits for them, and re-layouts: 3.5 us -> none
    convert_element_type x4 -> x0, other arithmetic: 2.16 us -> none  [the longest x2 1.14 us: residual_block_forward(): normed = (wide * inv * gain).astype(jnp.bfloat16)]
  transfers between devices with their start and end apart: 8 -> 0, of which waited for: 4 -> 0; matrix products, arithmetic and copies ran while one was open for 10% -> 0% of each run, Pallas kernels for 0% -> 0%
where the time goes in v1:
time: 69.6 us; the launch traced here: 68.5 us
  Pallas kernels  67.8 us (97%)
    pallas_call x1, Pallas kernels, per_device(): pl.pallas_call(make_kernel(devices, near, far, rows, chunks), out_shape=(...  66.1 us
    pallas_call x1, Pallas kernels, per_device(): pl.pallas_call(hand_over, out_shape=(block, block), in_specs=[vmem, vmem]...  1.78 us

profile of v1, /device:TPU:24, one launch (start us, length us, event | category | flops | bytes accessed | tf_op | source)
XLA Modules:
  0.0 68.5 jit_solution(13673938694643572222)
XLA Ops:
  0.6 66.1 %shard_map.113 = (bf16[128,768]{1,0:T(8,128)(2,1)}, bf16[128,768]{1,0:T(8,128)(2,1)}) custom-call(bf16[128,768]{1,0:T(8,128)(2,1)} %x_hbm.1, f32[768]{0:T(1024)} %g1_ref.1, bf16[3,768,768]{2,1,0:T(8,128)(2,1)} %w1_hbm.1, bf16[768,768]{1,0:T(8,128)(2,1)} %m1_hbm.1, bf16[768,768]{1,0:T(8,128)(2,1)} %p1_hbm.1, f32[768]{0:T(1024)} %g2_ref.1, ...), custom_call_target="tpu_custom_call" | custom-call | tf_op jit(solution)/shard_map/pallas_call | solution.py:253
  66.7 1.8 %shard_map.114 = (bf16[128,768]{1,0:T(8,128)(2,1)}, bf16[128,768]{1,0:T(8,128)(2,1)}) custom-call(bf16[128,768]{1,0:T(8,128)(2,1)} %get-tuple-element.4.a, bf16[128,768]{1,0:T(8,128)(2,1)} %get-tuple-element.5.b), custom_call_target="tpu_custom_call" | custom-call | tf_op jit(solution)/shard_map/pallas_call | solution.py:279

commit v2 on v1

--- a/solution.py
+++ b/solution.py
@@ -18,6 +18,8 @@
 PROJECT = (4, 9)
 
 NEAR_FWD, FAR_FWD, FAR_BWD, NEAR_BWD = range(4)
+
+DEPTH = {FAR_FWD: 1, FAR_BWD: 1}
 
 
 def dot(a, b):
@@ -105,10 +107,25 @@
             for _, receives, copy in copies(stage, c):
                 pl.when(receives)(copy.wait_recv)
 
+        def sent(stage, c):
+            for sends, _, copy in copies(stage, c):
+                pl.when(sends)(copy.wait_send)
+
+        def send_far(stage, c):
+            @pl.when(held[stage] & (c >= DEPTH[stage]))
+            def _():
+                sent(stage, c - DEPTH[stage])
+
+            send(stage, c)
+
         def all_sent(stage):
             def body(c, carry):
-                for sends, _, copy in copies(stage, c):
-                    pl.when(sends)(copy.wait_send)
+                waited = held[stage] & (c < chunks - DEPTH[stage]) if stage in held else False
+
+                @pl.when(jnp.logical_not(waited))
+                def _():
+                    sent(stage, c)
+
                 return carry
 
             lax.fori_loop(0, chunks, body, 0)
@@ -130,6 +147,9 @@
         def normalize(wide, gain):
             inv = lax.rsqrt(jnp.mean(wide * wide, axis=-1, keepdims=True) + EPS)
             return inv, (wide * inv * gain).astype(jnp.bfloat16)
+
+        lane, slab = lax.rem(me // (far // 4), 4), lax.rem(me // far, 4)
+        held = {FAR_FWD: ((lane == 1) | (lane == 2)), FAR_BWD: ((lane == 1) | (lane == 2))}
 
         loads[0].wait()
         inv, normed = normalize(x_v[...].astype(jnp.float32), gain1)
@@ -158,7 +178,7 @@
             inv, normed = normalize(result.astype(jnp.float32), gain2)
             inv2[at, :] = inv
             nrm2[1, at] = normed
-            send(FAR_FWD, c)
+            send_far(FAR_FWD, c)
 
         per_chunk(first_forward)
 
@@ -179,7 +199,7 @@
             grad_mid = (ghid2[at, :] * slope_mid).astype(jnp.bfloat16)
             grad_act = dot(grad_mid, wts_t[8])
             gp2[1, at] = (grad_act * slope_pre).astype(jnp.bfloat16)
-            send(FAR_BWD, c)
+            send_far(FAR_BWD, c)
 
             @pl.when(c == 0)
             def _():

time: 69.6 us -> 68.1 us (0.978)
  Pallas kernels: 67.8 us -> 66.2 us
    pallas_call x1, Pallas kernels: 66.1 us -> 64.4 us  [per_device(): pl.pallas_call(make_kernel(devices, near, far, rows, chunks), out_shape=(...]
where the time goes in v2:
time: 68.1 us; the launch traced here: 66.8 us
  Pallas kernels  66.2 us (97%)
    pallas_call x1, Pallas kernels, per_device(): pl.pallas_call(make_kernel(devices, near, far, rows, chunks), out_shape=(...  64.4 us
    pallas_call x1, Pallas kernels, per_device(): pl.pallas_call(hand_over, out_shape=(block, block), in_specs=[vmem, vmem]...  1.78 us

profile of v2, /device:TPU:24, one launch (start us, length us, event | category | flops | bytes accessed | tf_op | source)
XLA Modules:
  0.0 66.8 jit_solution(10080036885125410202)
XLA Ops:
  0.6 64.4 %shard_map.113 = (bf16[128,768]{1,0:T(8,128)(2,1)}, bf16[128,768]{1,0:T(8,128)(2,1)}) custom-call(bf16[128,768]{1,0:T(8,128)(2,1)} %x_hbm.1, f32[768]{0:T(1024)} %g1_ref.1, bf16[3,768,768]{2,1,0:T(8,128)(2,1)} %w1_hbm.1, bf16[768,768]{1,0:T(8,128)(2,1)} %m1_hbm.1, bf16[768,768]{1,0:T(8,128)(2,1)} %p1_hbm.1, f32[768]{0:T(1024)} %g2_ref.1, ...), custom_call_target="tpu_custom_call" | custom-call | tf_op jit(solution)/shard_map/pallas_call | solution.py:273
  65.0 1.8 %shard_map.114 = (bf16[128,768]{1,0:T(8,128)(2,1)}, bf16[128,768]{1,0:T(8,128)(2,1)}) custom-call(bf16[128,768]{1,0:T(8,128)(2,1)} %get-tuple-element.4.a, bf16[128,768]{1,0:T(8,128)(2,1)} %get-tuple-element.5.b), custom_call_target="tpu_custom_call" | custom-call | tf_op jit(solution)/shard_map/pallas_call | solution.py:299

commit v3 on v2

--- a/solution.py
+++ b/solution.py
@@ -39,10 +39,10 @@
     strides = (near, far, far, near)
 
     def kernel(
-        x_hbm, g1_ref, w1_hbm, m1_hbm, p1_hbm, g2_ref, w2_hbm, m2_hbm, p2_hbm, cot_hbm,
+        x_hbm, g1_hbm, w1_hbm, m1_hbm, p1_hbm, g2_hbm, w2_hbm, m2_hbm, p2_hbm, cot_hbm,
         out_hbm, gin_hbm,
         wts, wts_t, x_v, cot_v, nrm1, nrm2, gp2, gp1, x2, hid2, dy1, out_v, gin_v,
-        slope_pre1, slope_mid1, slope_pre2, slope_mid2, own, ghid2, inv1, inv2,
+        slope_pre1, slope_mid1, slope_pre2, slope_mid2, own, ghid2, inv1, inv2, g1_ref, g2_ref,
         load_sem, store_sem, send_sem, recv_sem,
     ):
         me = lax.axis_index("seq")
@@ -63,6 +63,7 @@
             return pltpu.make_async_copy(src, dst, load_sem.at[i])
 
         loads = [load(0, x_hbm, x_v)]
+        gains = [load(8, g1_hbm, g1_ref), load(9, g2_hbm, g2_ref)]
         loads.append(load(1, w1_hbm, wts.at[pl.ds(0, 3)]))
         loads.append(load(2, m1_hbm, wts.at[3]))
         loads.append(load(3, p1_hbm, wts.at[4]))
@@ -70,7 +71,7 @@
         loads.append(load(5, p2_hbm, wts.at[9]))
         loads.append(load(6, m2_hbm, wts.at[8]))
         loads.append(load(7, w2_hbm, wts.at[pl.ds(5, 3)]))
-        for one in loads:
+        for one in gains + loads:
             one.start()
 
         for stage in range(4):
@@ -141,17 +142,18 @@
             for i in which:
                 wts_t[i] = wts[i].T
 
-        gain1 = g1_ref[...].reshape(1, C)
-        gain2 = g2_ref[...].reshape(1, C)
 
         def normalize(wide, gain):
             inv = lax.rsqrt(jnp.mean(wide * wide, axis=-1, keepdims=True) + EPS)
             return inv, (wide * inv * gain).astype(jnp.bfloat16)
 
         lane, slab = lax.rem(me // (far // 4), 4), lax.rem(me // far, 4)
-        held = {FAR_FWD: ((lane == 1) | (lane == 2)), FAR_BWD: ((lane == 1) | (lane == 2))}
-
-        loads[0].wait()
+        held = {FAR_FWD: ((lane == 1) | (lane == 2)), FAR_BWD: ((lane == 1) | (lane == 2)) | (lax.rem(me, 2) == 1)}
+
+        for one in gains + loads[:1]:
+            one.wait()
+        gain1 = g1_ref[...].reshape(1, C)
+        gain2 = g2_ref[...].reshape(1, C)
         inv, normed = normalize(x_v[...].astype(jnp.float32), gain1)
         inv1[...] = inv
         nrm1[1] = normed
@@ -273,7 +275,7 @@
         results = pl.pallas_call(
             make_kernel(devices, near, far, rows, chunks),
             out_shape=(block, block),
-            in_specs=[whole, vmem, whole, whole, whole, vmem, whole, whole, whole, whole],
+            in_specs=[whole] * 10,
             out_specs=(whole, whole),
             scratch_shapes=[
                 pltpu.VMEM((10, C, C), jnp.bfloat16),
@@ -282,7 +284,9 @@
                 f32(), f32(), f32(), f32(), f32(), f32(),
                 pltpu.VMEM((rows, 1), jnp.float32),
                 pltpu.VMEM((rows, 1), jnp.float32),
-                pltpu.SemaphoreType.DMA((8,)),
+                pltpu.VMEM((C,), jnp.float32),
+                pltpu.VMEM((C,), jnp.float32),
+                pltpu.SemaphoreType.DMA((10,)),
                 pltpu.SemaphoreType.DMA((2,)),
                 pltpu.SemaphoreType.DMA((4, 2, chunks)),
                 pltpu.SemaphoreType.DMA((4, 2, chunks)),

time: 68.1 us -> 66.9 us (0.982)
  Pallas kernels: 66.2 us -> 65.1 us
    pallas_call x1, Pallas kernels: 64.4 us -> 63.3 us  [per_device(): pl.pallas_call(make_kernel(devices, near, far, rows, chunks), out_shape=(...]
where the time goes in v3:
time: 66.9 us; the launch traced here: 65.7 us
  Pallas kernels  65.1 us (97%)
    pallas_call x1, Pallas kernels, per_device(): pl.pallas_call(make_kernel(devices, near, far, rows, chunks), out_shape=(...  63.3 us
    pallas_call x1, Pallas kernels, per_device(): pl.pallas_call(hand_over, out_shape=(block, block), in_specs=[vmem, vmem]...  1.78 us

profile of v3, /device:TPU:24, one launch (start us, length us, event | category | flops | bytes accessed | tf_op | source)
XLA Modules:
  0.0 65.7 jit_solution(6484537337699421591)
XLA Ops:
  0.6 63.3 %shard_map.113 = (bf16[128,768]{1,0:T(8,128)(2,1)}, bf16[128,768]{1,0:T(8,128)(2,1)}) custom-call(bf16[128,768]{1,0:T(8,128)(2,1)} %x_hbm.1, f32[768]{0:T(1024)} %g1_hbm.1, bf16[3,768,768]{2,1,0:T(8,128)(2,1)} %w1_hbm.1, bf16[768,768]{1,0:T(8,128)(2,1)} %m1_hbm.1, bf16[768,768]{1,0:T(8,128)(2,1)} %p1_hbm.1, f32[768]{0:T(1024)} %g2_hbm.1, ...), custom_call_target="tpu_custom_call" | custom-call | tf_op jit(solution)/shard_map/pallas_call | solution.py:275
  64.0 1.8 %shard_map.114 = (bf16[128,768]{1,0:T(8,128)(2,1)}, bf16[128,768]{1,0:T(8,128)(2,1)}) custom-call(bf16[128,768]{1,0:T(8,128)(2,1)} %get-tuple-element.4.a, bf16[128,768]{1,0:T(8,128)(2,1)} %get-tuple-element.5.b), custom_call_target="tpu_custom_call" | custom-call | tf_op jit(solution)/shard_map/pallas_call | solution.py:303

commit v4 on v3

--- a/solution.py
+++ b/solution.py
@@ -51,14 +51,6 @@
         def exists(distance):
             return (me + distance >= 0) & (me + distance < devices)
 
-        barrier = pltpu.get_barrier_semaphore()
-        partners = (-near, near, -far, far)
-        for distance in partners:
-
-            @pl.when(exists(distance))
-            def _():
-                pl.semaphore_signal(barrier, inc=1, device_id=(me + distance,), device_id_type=MESH)
-
         def load(i, src, dst):
             return pltpu.make_async_copy(src, dst, load_sem.at[i])
 
@@ -71,7 +63,18 @@
         loads.append(load(5, p2_hbm, wts.at[9]))
         loads.append(load(6, m2_hbm, wts.at[8]))
         loads.append(load(7, w2_hbm, wts.at[pl.ds(5, 3)]))
-        for one in gains + loads:
+        for one in loads[:1] + gains:
+            one.start()
+
+        barrier = pltpu.get_barrier_semaphore()
+        partners = (-near, near, -far, far)
+        for distance in partners:
+
+            @pl.when(exists(distance))
+            def _():
+                pl.semaphore_signal(barrier, inc=1, device_id=(me + distance,), device_id_type=MESH)
+
+        for one in loads[1:]:
             one.start()
 
         for stage in range(4):

time: 66.9 us -> 66.9 us (level)
  no operation moved by 1% of the time
where the time goes in v4:
time: 66.9 us; the launch traced here: 65.7 us
  Pallas kernels  65.1 us (97%)
    pallas_call x1, Pallas kernels, per_device(): pl.pallas_call(make_kernel(devices, near, far, rows, chunks), out_shape=(...  63.3 us
    pallas_call x1, Pallas kernels, per_device(): pl.pallas_call(hand_over, out_shape=(block, block), in_specs=[vmem, vmem]...  1.78 us

profile of v4, /device:TPU:24, one launch (start us, length us, event | category | flops | bytes accessed | tf_op | source)
XLA Modules:
  0.0 65.7 jit_solution(7310374994842727450)
XLA Ops:
  0.6 63.3 %shard_map.113 = (bf16[128,768]{1,0:T(8,128)(2,1)}, bf16[128,768]{1,0:T(8,128)(2,1)}) custom-call(bf16[128,768]{1,0:T(8,128)(2,1)} %x_hbm.1, f32[768]{0:T(1024)} %g1_hbm.1, bf16[3,768,768]{2,1,0:T(8,128)(2,1)} %w1_hbm.1, bf16[768,768]{1,0:T(8,128)(2,1)} %m1_hbm.1, bf16[768,768]{1,0:T(8,128)(2,1)} %p1_hbm.1, f32[768]{0:T(1024)} %g2_hbm.1, ...), custom_call_target="tpu_custom_call" | custom-call | tf_op jit(solution)/shard_map/pallas_call | solution.py:278
  64.0 1.8 %shard_map.114 = (bf16[128,768]{1,0:T(8,128)(2,1)}, bf16[128,768]{1,0:T(8,128)(2,1)}) custom-call(bf16[128,768]{1,0:T(8,128)(2,1)} %get-tuple-element.4.a, bf16[128,768]{1,0:T(8,128)(2,1)} %get-tuple-element.5.b), custom_call_target="tpu_custom_call" | custom-call | tf_op jit(solution)/shard_map/pallas_call | solution.py:306
